TPU v7x, 256 devices: a whole 4x4x8 slice. The times are simulated.
256 devices in a mesh: space: 32 (over z_lo, y, core), fac: 8 (over z_hi, x).
Axes of the slice: x: 4, y: 4, z: 8 (z_hi: 2, z_lo: 4; z = z_hi * 4 + z_lo), core: 2. Of those that a mesh axis runs over, the one named last changes fastest.
Arguments:
- activations: bfloat16 [8, 64, 16, 16, 128], P('fac', 'space'), may hold values from -60 to 60
- out_grad: bfloat16 [8, 64, 16, 16, 128], P('fac', 'space'), may hold values from -60 to 60
- kernel: bfloat16 [27, 128, 128], replicated, may hold values from -0.109375 to 0.109375
Outputs:
- in_grad: bfloat16 [8, 64, 16, 16, 128], P('fac', 'space')
- update: float32 [27, 128, 128], P(None, 'fac')
All inputs are finite; a program needn't handle non-finite values.
Results may differ from a plain program's by a relative error of at most 0.0014.
Values may be sent and summed in bfloat16 or wider, within the bound.
No kernel may reach another device: no remote copies, remote signals or barrier semaphores. Data moves between devices by JAX's collectives and lax.ppermute only.
A program may use at most 128 MiB of HBM per device.

v0:
```python
import math
import jax
import jax.numpy as jnp
from jax import lax
from jax.sharding import PartitionSpec as P

damping = 0.1
clip_rate = 0.05


def with_halo(cells, sides, width):
    for axis, dim in sides:
        count = lax.axis_size(axis)
        ends = count - 1
        head = lax.slice_in_dim(cells, 0, width, axis=dim)
        tail = lax.slice_in_dim(cells, cells.shape[dim] - width, cells.shape[dim], axis=dim)
        cells = jnp.concatenate(
            [
                lax.ppermute(tail, axis, [(i, (i + 1) % count) for i in range(ends)]),
                cells,
                lax.ppermute(head, axis, [((i + 1) % count, i) for i in range(ends)]),
            ],
            axis=dim,
        )
    return cells


def offsets():
    return [(a, b, c) for a in (-1, 0, 1) for b in (-1, 0, 1) for c in (-1, 0, 1)]


def window(padded, shift, extent):
    return padded[
        1 + shift[0] : 1 + shift[0] + extent[0],
        1 + shift[1] : 1 + shift[1] + extent[1],
        1 + shift[2] : 1 + shift[2] + extent[2],
    ]


def local_stats(padded_in, rows_cot, extent, groups):
    cells = rows_cot.shape[0]
    width = padded_in.shape[-1] // groups
    gram_list = []
    grad_list = []
    for block_index in range(groups):
        lower = block_index * width
        pieces = [
            window(padded_in, shift, extent)[..., lower : lower + width].reshape(cells, width)
            for shift in offsets()
        ]
        patch = jnp.concatenate(pieces, axis=1)
        gram_list.append(jnp.dot(patch.T, patch, preferred_element_type=jnp.float32))
        grad_list.append(jnp.dot(patch.T, rows_cot, preferred_element_type=jnp.float32))
    grads = jnp.stack(grad_list)
    return (jnp.stack(gram_list), grads)


def on_device(activations, out_grad, kernel):
    inputs = activations[0]
    cotangent = out_grad[0]
    size_x, size_y, size_z, channels = inputs.shape
    extent = (size_x, size_y, size_z)
    cells = size_x * size_y * size_z
    groups = lax.axis_size("fac")
    width = channels // groups
    stacked = jnp.concatenate([inputs, cotangent], axis=3)
    rimmed = with_halo(stacked, (("space", 0),), 1)
    padded = jnp.pad(rimmed, ((0, 0), (1, 1), (1, 1), (0, 0)))
    padded_in = padded[..., :channels]
    padded_cot = padded[..., channels:]
    rows_cot = cotangent.reshape(cells, channels)
    cot_gram = jnp.dot(rows_cot.T, rows_cot, preferred_element_type=jnp.float32)
    in_grad = jnp.zeros((cells, channels), jnp.float32)
    for tap_index, shift in enumerate(offsets()):
        back = (-shift[0], -shift[1], -shift[2])
        rows = window(padded_cot, back, extent).reshape(cells, channels)
        in_grad = in_grad + jnp.dot(rows, kernel[tap_index].T, preferred_element_type=jnp.float32)
    in_grad = in_grad.astype(jnp.bfloat16).reshape(activations.shape)
    cot_total = lax.psum(cot_gram, ("space", "fac"))
    grams, grads = local_stats(padded_in, rows_cot, extent, groups)
    summed = lax.psum((grams, grads), "space")
    owned = (
        lax.psum_scatter(summed[0], "fac", scatter_dimension=0, tiled=True),
        lax.psum_scatter(summed[1], "fac", scatter_dimension=0, tiled=True),
    )
    gram_block = owned[0][0]
    grad_block = owned[1][0]
    count = float(cells * lax.axis_size("space") * groups)
    order = gram_block.shape[0]
    right_mat = cot_total / count + damping * jnp.eye(channels, dtype=jnp.float32)
    right_chol = jnp.linalg.cholesky(right_mat)
    left_mat = gram_block / count + damping * jnp.eye(order, dtype=jnp.float32)
    left_chol = jnp.linalg.cholesky(left_mat)
    scaled = grad_block / math.sqrt(count)
    half = jax.scipy.linalg.cho_solve((left_chol, True), scaled)
    raw = jax.scipy.linalg.cho_solve((right_chol, True), half.T).T
    total = lax.psum(jnp.sum(raw * scaled), "fac")
    factor = jnp.sqrt(clip_rate * kernel.size / total)
    update = raw.reshape(27, width, channels) * factor
    return (in_grad, update)


def solution(mesh):
    placed = (P("fac", "space", None, None, None), P("fac", "space", None, None, None), P())
    return jax.shard_map(
        on_device,
        mesh=mesh,
        in_specs=placed,
        out_specs=(P("fac", "space", None, None, None), P(None, "fac", None)),
        check_vma=False,
    )
```

profile of v0, /device:TPU:0, one launch (start us, length us, event | category | flops | bytes accessed | tf_op | source)
XLA Modules:
  0.0 795.9 jit_solution(12100450884241944340)
XLA Ops:
  8.1 1.9 convolution_bitcast_fusion.16
  16.7 1.6 fusion.150
  18.4 1.7 fusion.154
  20.1 2.2 fusion.152
  22.3 2.3 fusion.148
  24.6 2.3 fusion.149
  26.9 2.2 fusion.146
  29.1 2.2 fusion.153
  31.3 2.3 fusion.147
  33.6 2.2 fusion.151
  35.8 2.2 fusion.145
  38.1 1.9 fusion.158
  40.0 3.3 concatenate.80
  44.4 3.4 concatenate.81
  48.8 3.3 concatenate.82
  53.1 3.4 concatenate.83
  57.4 4.2 concatenate.84
  61.7 2.1 fusion.14
  63.7 4.2 concatenate.85
  68.0 2.1 fusion.13
  70.0 4.2 concatenate.86
  74.3 2.1 fusion.12
  76.3 4.2 concatenate.87
  80.6 2.0 fusion.11
  82.7 1.4 fusion.10
  84.0 1.4 fusion.9
  86.8 1.4 fusion.7
  90.8 1.4 fusion.4
  94.5 214.7 %all-reduce.8.cloned.1.call-done = f32[128,128]{1,0:T(8,128)} async-done(((f32[128,128]{1,0:T(8,128)}), f32[128,128]{1,0:T(8,128)}) %all-reduce.8.cloned.1.call-update) | async-done | bytes 65552 | tf_op jit(solution)/shard_map/psum | solution.py:79
  311.0 11.7 %cholesky.100 = f32[128,128]{1,0:T(8,128)S(1)} custom-call(f32[128,128]{1,0:T(8,128)S(1)} %fusion.73), custom_call_target="Cholesky" | custom-call | tf_op jit(solution)/shard_map/jit(cholesky)/cholesky | solution.py:91
  324.0 10.4 %custom-call.44 = f32[1,128,128]{1,2,0:T(8,128)} custom-call(f32[1,128,128]{2,1,0:T(8,128)S(1)} %fusion.62), custom_call_target="InvertDiagBlocksLowerTriangular" | custom-call | tf_op jit(solution)/shard_map/jit(_cho_solve)/triangular_solve | solution.py:96
  334.5 1.6 slice.1801
  340.9 9.6 %reduce-scatter.3.cloned.1.call-done = f32[1,432,432]{2,1,0:T(8,128)} async-done(((f32[8,432,432]{2,1,0:T(8,128)}), f32[1,432,432]{2,1,0:T(8,128)}) %reduce-scatter.3.cloned.1.call-update) | async-done | bytes 746512 | tf_op jit(solution)/shard_map/reduce_scatter | solution.py:83
  352.1 268.3 %all-reduce.10.cloned.1.call-done = (f32[1,432,432]{2,1,0:T(8,128)}, f32[1,432,128]{2,1,0:T(8,128)}) async-done(((f32[1,432,432]{2,1,0:T(8,128)}, f32[1,432,128]{2,1,0:T(8,128)}), (f32[1,432,432]{2,1,0:T(8,128)}, f32[1,432,128]{2,1,0:T(8,128)})) %all-reduce.10.cloned.1.call-update) | async-done | bytes 967696 | tf_op jit(solution)/shard_map/psum | solution.py:81
  621.4 1.4 bitcast_add_fusion.1
  623.3 12.1 %cholesky.109 = f32[128,128]{1,0:T(8,128)S(1)} custom-call(f32[128,128]{1,0:T(8,128)S(1)} %cholesky.264), custom_call_target="Cholesky" | custom-call | tf_op jit(solution)/shard_map/jit(cholesky)/cholesky | solution.py:93
  636.2 9.8 %custom-call.45 = f32[1,128,128]{1,2,0:T(8,128)S(1)} custom-call(f32[1,128,128]{2,1,0:T(8,128)S(1)} %get-tuple-element.273), custom_call_target="InvertDiagBlocksLowerTriangular" | custom-call | tf_op jit(solution)/shard_map/jit(cholesky)/cholesky | solution.py:93
  648.6 11.7 %cholesky.212 = f32[128,128]{1,0:T(8,128)S(1)} custom-call(f32[128,128]{1,0:T(8,128)S(1)} %cholesky.268), custom_call_target="Cholesky" | custom-call | tf_op jit(solution)/shard_map/jit(cholesky)/cholesky | solution.py:93
  661.0 9.8 %custom-call.46 = f32[1,128,128]{1,2,0:T(8,128)S(1)} custom-call(f32[1,128,128]{2,1,0:T(8,128)S(1)} %get-tuple-element.270), custom_call_target="InvertDiagBlocksLowerTriangular" | custom-call | tf_op jit(solution)/shard_map/jit(cholesky)/cholesky | solution.py:93
  672.3 11.9 %cholesky.233 = f32[128,128]{1,0:T(8,128)S(1)} custom-call(f32[128,128]{1,0:T(8,128)S(1)} %cholesky.273), custom_call_target="Cholesky" | custom-call | tf_op jit(solution)/shard_map/jit(cholesky)/cholesky | solution.py:93
  684.8 9.8 %custom-call.47 = f32[1,128,128]{1,2,0:T(8,128)S(1)} custom-call(f32[1,128,128]{2,1,0:T(8,128)S(1)} %get-tuple-element.267), custom_call_target="InvertDiagBlocksLowerTriangular" | custom-call | tf_op jit(solution)/shard_map/jit(cholesky)/cholesky | solution.py:93
  695.8 4.4 cholesky.253
  703.5 6.1 while.1
  704.2 1.4 bitcast_dynamic-update-slice_fusion.2
  706.2 1.4 bitcast_dynamic-update-slice_fusion.2
  708.2 1.4 bitcast_dynamic-update-slice_fusion.2
  709.8 39.3 %custom-call.48 = f32[4,128,128]{1,2,0:T(8,128)S(1)} custom-call(f32[4,128,128]{2,1,0:T(8,128)S(1)} %pad_maximum_fusion.1), custom_call_target="InvertDiagBlocksLowerTriangular" | custom-call | tf_op jit(solution)/shard_map/jit(_cho_solve)/triangular_solve | solution.py:95
  754.6 32.0 %psum.31 = f32[]{:T(128)} all-reduce(f32[]{:T(128)} %get-tuple-element.278), channel_id=1, replica_groups=mesh['space'=32,'fac'=8] {'fac'}, use_global_device_ids=true, to_apply=%region_16.17 | all-reduce | flops 1 | bytes 8 | tf_op jit(solution)/shard_map/psum | solution.py:97
  (147 shorter events, 44.4 us)
Async XLA Ops:
  8.0 7.6 copy-start
  8.0 5.6 copy-start.1
  8.0 301.1 %all-reduce.8.cloned.1.call-start = ((), (), s32[]{:S(2)}) async-start(), calls=%async_computation.2 | async-start | bytes 131072 | tf_op jit(solution)/shard_map/psum | solution.py:79
  9.9 330.9 %reduce-scatter.5.cloned.1.call-start = ((), (), s32[]{:S(2)}) async-start(), calls=%async_computation.4 | async-start | bytes 1990656 | tf_op jit(solution)/shard_map/reduce_scatter | solution.py:84
  11.0 3.8 collective-permute-start
  12.3 3.3 collective-permute-start.1
  38.1 1.9 copy-start.6
  44.4 4.4 copy-start.11
  82.6 267.9 %reduce-scatter.3.cloned.1.call-start = ((), (), s32[]{:S(2)}) async-start(), calls=%async_computation.3 | async-start | bytes 7962624 | tf_op jit(solution)/shard_map/reduce_scatter | solution.py:83
  85.4 2.7 copy-start.2
  86.8 2.7 copy-start.3
  88.1 2.7 copy-start.4
  89.5 2.7 copy-start.5
  93.6 242.6 %copy-start.10 = (bf16[27,128,128]{2,1,0:T(8,128)(2,1)S(1)}, bf16[27,128,128]{2,1,0:T(8,128)(2,1)}, u32[]{:S(2)}) copy-start(bf16[27,128,128]{2,1,0:T(8,128)(2,1)} %param.5) | copy-start | bytes 2654212
  93.6 526.9 %all-reduce.10.cloned.1.call-start = ((), (), s32[]{:S(2)}) async-start(), calls=%async_computation.5 | async-start | bytes 2211840 | tf_op jit(solution)/shard_map/psum | solution.py:81
  340.0 10.5 %copy-start.12 = (bf16[2,16,16,128]{3,2,1,0:T(8,128)(2,1)S(1)}, bf16[2,16,16,128]{3,2,1,0:T(8,128)(2,1)}, u32[]{:S(2)}) copy-start(bf16[2,16,16,128]{3,2,1,0:T(8,128)(2,1)} %slice.1801) | copy-start | bytes 393220
  621.4 1.7 copy-start.7
  623.3 12.9 %copy-start.8 = (f32[432,432]{1,0:T(8,128)}, f32[432,432]{1,0:T(8,128)S(1)}, u32[]{:S(2)}) copy-start(f32[432,432]{1,0:T(8,128)S(1)} %fusion.25) | copy-start | bytes 2239492
  648.5 55.0 %copy-start.15 = (f32[3,128,128]{2,1,0:T(8,128)S(1)}, f32[3,128,128]{2,1,0:T(8,128)}, u32[]{:S(2)}) copy-start(f32[3,128,128]{2,1,0:T(8,128)} %custom-call.51) | copy-start | bytes 589828
  672.2 37.4 %copy-start.13 = (f32[128,80]{1,0:T(8,128)S(1)}, f32[128,80]{1,0:T(8,128)}, u32[]{:S(2)}) copy-start(f32[128,80]{1,0:T(8,128)} %pad_convert_fusion) | copy-start | bytes 122884
  709.7 43.3 %copy-start.14 = (f32[1,128,128]{1,2,0:T(8,128)S(1)}, f32[1,128,128]{1,2,0:T(8,128)}, u32[]{:S(2)}) copy-start(f32[1,128,128]{1,2,0:T(8,128)} %custom-call.44) | copy-start | bytes 196612
  749.4 4.1 copy-start.9
Sparse Core Ops, SparseCore 0:
  14.4 294.7 all-reduce.7
Sparse Core Ops, SparseCore 1:
  82.7 99.6 reduce-scatter.4
  186.6 163.9 reduce-scatter.2
  353.3 267.1 all-reduce.9
where the time goes:
time: 806 us; the launch traced here: 796 us
  waiting for transfers between devices  494 us (61%)
  other arithmetic  142 us (18%)
  local copies, waits for them, and re-layouts  64 us (8%)
  matrix products  41.1 us (5%)
  blocking collectives  32 us (4%)
  between operations  19.9 us (2%)
    psum x1, waiting for transfers between devices, on_device(): summed = lax.psum((grams, grads), 'space')  268 us
    psum x1, waiting for transfers between devices, on_device(): cot_total = lax.psum(cot_gram, ('space', 'fac'))  215 us
    another operation x15, other arithmetic, on_device(): left_chol = jnp.linalg.cholesky(left_mat)  72.3 us
    another operation x7, other arithmetic, on_device(): half = jax.scipy.linalg.cho_solve((left_chol, True), scaled)  40.2 us
    psum x1, blocking collectives, on_device(): total = lax.psum(jnp.sum(raw * scaled), 'fac')  32 us
    concatenate x8, local copies, waits for them, and re-layouts, local_stats(): patch = jnp.concatenate(pieces, axis=1)  30.3 us
    slice x13, local copies, waits for them, and re-layouts, local_stats(): window(padded_in, shift, extent)[..., lower:lower + width]  25.1 us
  transfers between devices with their start and end apart: 6, of which 4 were waited for; matrix products, arithmetic and copies ran while one was open for 14% of the time, Pallas kernels for 0%

commit v1 on v0

--- a/solution.py
+++ b/solution.py
@@ -76,7 +76,7 @@
         rows = window(padded_cot, back, extent).reshape(cells, channels)
         in_grad = in_grad + jnp.dot(rows, kernel[tap_index].T, preferred_element_type=jnp.float32)
     in_grad = in_grad.astype(jnp.bfloat16).reshape(activations.shape)
-    cot_total = lax.psum(cot_gram, ("space", "fac"))
+    cot_total = lax.psum(lax.psum(cot_gram, "fac"), "space")
     grams, grads = local_stats(padded_in, rows_cot, extent, groups)
     summed = lax.psum((grams, grads), "space")
     owned = (

time: 806 us -> 861 us (1.068)
  waiting for transfers between devices: 494 us -> 551 us
    psum x1, waiting for transfers between devices: 215 us -> 17.3 us  [on_device(): cot_total = lax.psum(lax.psum(cot_gram, 'fac'), 'space')]
    reduce_scatter x1, waiting for transfers between devices: 9.63 us -> 169 us  [on_device(): lax.psum_scatter(summed[0], 'fac', scatter_dimension=0, tiled=True)]
    reduce_scatter x1, waiting for transfers between devices: 0.03 us -> 92.4 us  [on_device(): lax.psum_scatter(summed[1], 'fac', scatter_dimension=0, tiled=True)]
  transfers between devices with their start and end apart: 6 -> 6, of which waited for: 4 -> 5; matrix products, arithmetic and copies ran while one was open for 14% -> 10% of each run, Pallas kernels for 0% -> 0%
where the time goes in v1:
time: 861 us; the launch traced here: 851 us
  waiting for transfers between devices  551 us (64%)
  other arithmetic  142 us (16%)
  local copies, waits for them, and re-layouts  64.3 us (7%)
  matrix products  41.1 us (5%)
  blocking collectives  32 us (4%)
  between operations  18.1 us (2%)
    psum x1, waiting for transfers between devices, on_device(): summed = lax.psum((grams, grads), 'space')  271 us
    reduce_scatter x1, waiting for transfers between devices, on_device(): lax.psum_scatter(summed[0], 'fac', scatter_dimension=0, tiled=True)  169 us
    reduce_scatter x1, waiting for transfers between devices, on_device(): lax.psum_scatter(summed[1], 'fac', scatter_dimension=0, tiled=True)  92.4 us
    another operation x15, other arithmetic, on_device(): left_chol = jnp.linalg.cholesky(left_mat)  72.4 us
    another operation x7, other arithmetic, on_device(): half = jax.scipy.linalg.cho_solve((left_chol, True), scaled)  40.2 us
    psum x1, blocking collectives, on_device(): total = lax.psum(jnp.sum(raw * scaled), 'fac')  32 us
    concatenate x8, local copies, waits for them, and re-layouts, local_stats(): patch = jnp.concatenate(pieces, axis=1)  30.3 us
    slice x13, local copies, waits for them, and re-layouts, local_stats(): window(padded_in, shift, extent)[..., lower:lower + width]  25.2 us
  transfers between devices with their start and end apart: 6, of which 5 were waited for; matrix products, arithmetic and copies ran while one was open for 10% of the time, Pallas kernels for 0%

profile of v1, /device:TPU:0, one launch (start us, length us, event | category | flops | bytes accessed | tf_op | source)
XLA Modules:
  0.0 851.1 jit_solution(4234133339242041363)
XLA Ops:
  7.2 1.9 convolution_bitcast_fusion.16
  15.9 1.6 fusion.150
  17.6 1.7 fusion.154
  19.3 2.2 fusion.152
  21.5 2.3 fusion.148
  23.8 2.3 fusion.149
  26.1 2.2 fusion.146
  28.3 2.3 fusion.153
  30.5 2.3 fusion.147
  32.8 2.3 fusion.151
  35.1 2.3 fusion.145
  37.4 1.9 fusion.158
  39.3 3.3 concatenate.80
  43.7 3.4 concatenate.81
  48.1 3.3 concatenate.82
  52.4 3.4 concatenate.83
  56.8 4.2 concatenate.84
  61.0 2.0 fusion.14
  63.0 4.2 concatenate.85
  67.3 2.1 fusion.13
  69.3 4.2 concatenate.86
  73.5 2.1 fusion.12
  75.6 4.2 concatenate.87
  79.8 2.0 fusion.11
  81.9 1.4 fusion.10
  83.3 1.4 fusion.9
  90.1 1.4 fusion.4
  93.8 1.6 slice.1801
  100.2 17.3 %all-reduce.8.cloned.1.call-done = f32[128,128]{1,0:T(8,128)} async-done(((f32[128,128]{1,0:T(8,128)}), f32[128,128]{1,0:T(8,128)}) %all-reduce.8.cloned.1.call-update) | async-done | bytes 65552 | tf_op jit(solution)/shard_map/psum | solution.py:79
  117.5 92.4 %reduce-scatter.5.cloned.1.call-done = f32[1,432,128]{2,1,0:T(8,128)} async-done(((f32[8,432,128]{2,1,0:T(8,128)}), f32[1,432,128]{2,1,0:T(8,128)}) %reduce-scatter.5.cloned.1.call-update) | async-done | bytes 221200 | tf_op jit(solution)/shard_map/reduce_scatter | solution.py:84
  209.9 168.9 %reduce-scatter.3.cloned.1.call-done = f32[1,432,432]{2,1,0:T(8,128)} async-done(((f32[8,432,432]{2,1,0:T(8,128)}), f32[1,432,432]{2,1,0:T(8,128)}) %reduce-scatter.3.cloned.1.call-update) | async-done | bytes 746512 | tf_op jit(solution)/shard_map/reduce_scatter | solution.py:83
  380.4 271.2 %all-reduce.10.cloned.1.call-done = (f32[1,432,432]{2,1,0:T(8,128)}, f32[1,432,128]{2,1,0:T(8,128)}, f32[128,128]{1,0:T(8,128)}) async-done(((f32[1,432,432]{2,1,0:T(8,128)}, f32[1,432,128]{2,1,0:T(8,128)}, f32[128,128]{1,0:T(8,128)}), (f32[1,432,432]{2,1,0:T(8,128)}, f32[1,432,128]{2,1,0:T(8,128)}, f32[128,128]{1,0:T(8,128)})) %all-reduce.10.cloned.1.call-update) | async-done | bytes 1033232 | tf_op jit(solution)/shard_map/psum | solution.py:81
  653.5 11.7 %cholesky.100 = f32[128,128]{1,0:T(8,128)S(1)} custom-call(f32[128,128]{1,0:T(8,128)S(1)} %fusion.73), custom_call_target="Cholesky" | custom-call | tf_op jit(solution)/shard_map/jit(cholesky)/cholesky | solution.py:91
  666.6 9.8 %custom-call.44 = f32[1,128,128]{1,2,0:T(8,128)S(1)} custom-call(f32[1,128,128]{2,1,0:T(8,128)S(1)} %fusion.62), custom_call_target="InvertDiagBlocksLowerTriangular" | custom-call | tf_op jit(solution)/shard_map/jit(_cho_solve)/triangular_solve | solution.py:96
  677.4 1.4 bitcast_add_fusion.1
  679.3 12.1 %cholesky.109 = f32[128,128]{1,0:T(8,128)S(1)} custom-call(f32[128,128]{1,0:T(8,128)S(1)} %cholesky.264), custom_call_target="Cholesky" | custom-call | tf_op jit(solution)/shard_map/jit(cholesky)/cholesky | solution.py:93
  692.1 9.8 %custom-call.45 = f32[1,128,128]{1,2,0:T(8,128)S(1)} custom-call(f32[1,128,128]{2,1,0:T(8,128)S(1)} %get-tuple-element.274), custom_call_target="InvertDiagBlocksLowerTriangular" | custom-call | tf_op jit(solution)/shard_map/jit(cholesky)/cholesky | solution.py:93
  704.5 11.7 %cholesky.212 = f32[128,128]{1,0:T(8,128)S(1)} custom-call(f32[128,128]{1,0:T(8,128)S(1)} %cholesky.268), custom_call_target="Cholesky" | custom-call | tf_op jit(solution)/shard_map/jit(cholesky)/cholesky | solution.py:93
  717.0 9.8 %custom-call.46 = f32[1,128,128]{1,2,0:T(8,128)S(1)} custom-call(f32[1,128,128]{2,1,0:T(8,128)S(1)} %get-tuple-element.271), custom_call_target="InvertDiagBlocksLowerTriangular" | custom-call | tf_op jit(solution)/shard_map/jit(cholesky)/cholesky | solution.py:93
  728.2 11.9 %cholesky.233 = f32[128,128]{1,0:T(8,128)S(1)} custom-call(f32[128,128]{1,0:T(8,128)S(1)} %cholesky.273), custom_call_target="Cholesky" | custom-call | tf_op jit(solution)/shard_map/jit(cholesky)/cholesky | solution.py:93
  740.9 9.8 %custom-call.47 = f32[1,128,128]{1,2,0:T(8,128)S(1)} custom-call(f32[1,128,128]{2,1,0:T(8,128)S(1)} %get-tuple-element.268), custom_call_target="InvertDiagBlocksLowerTriangular" | custom-call | tf_op jit(solution)/shard_map/jit(cholesky)/cholesky | solution.py:93
  751.8 4.4 cholesky.253
  759.7 6.2 while.1
  760.4 1.4 bitcast_dynamic-update-slice_fusion.2
  762.5 1.4 bitcast_dynamic-update-slice_fusion.2
  764.6 1.4 bitcast_dynamic-update-slice_fusion.2
  766.1 39.3 %custom-call.48 = f32[4,128,128]{1,2,0:T(8,128)S(1)} custom-call(f32[4,128,128]{2,1,0:T(8,128)S(1)} %pad_maximum_fusion.1), custom_call_target="InvertDiagBlocksLowerTriangular" | custom-call | tf_op jit(solution)/shard_map/jit(_cho_solve)/triangular_solve | solution.py:95
  811.0 32.0 %psum.39 = f32[]{:T(128)} all-reduce(f32[]{:T(128)} %get-tuple-element.279), channel_id=1, replica_groups=mesh['space'=32,'fac'=8] {'fac'}, use_global_device_ids=true, to_apply=%region_17.18 | all-reduce | flops 1 | bytes 8 | tf_op jit(solution)/shard_map/psum | solution.py:97
  (145 shorter events, 45.9 us)
Async XLA Ops:
  7.2 7.6 copy-start
  7.2 5.6 copy-start.1
  7.2 110.3 %all-reduce.8.cloned.1.call-start = ((), (), s32[]{:S(2)}) async-start(), calls=%async_computation.2 | async-start | bytes 131072 | tf_op jit(solution)/shard_map/psum | solution.py:79
  9.1 200.8 %reduce-scatter.5.cloned.1.call-start = ((), (), s32[]{:S(2)}) async-start(), calls=%async_computation.4 | async-start | bytes 1990656 | tf_op jit(solution)/shard_map/reduce_scatter | solution.py:84
  10.1 3.8 collective-permute-start
  11.4 3.3 collective-permute-start.1
  37.4 1.9 copy-start.6
  43.7 4.4 copy-start.11
  81.9 296.9 %reduce-scatter.3.cloned.1.call-start = ((), (), s32[]{:S(2)}) async-start(), calls=%async_computation.3 | async-start | bytes 7962624 | tf_op jit(solution)/shard_map/reduce_scatter | solution.py:83
  84.7 2.7 copy-start.2
  86.0 2.7 copy-start.3
  87.4 2.7 copy-start.4
  88.7 2.7 copy-start.5
  92.8 2.6 copy-start.10
  92.8 558.8 %all-reduce.10.cloned.1.call-start = ((), (), s32[]{:S(2)}) async-start(), calls=%async_computation.5 | async-start | bytes 2342912 | tf_op jit(solution)/shard_map/psum | solution.py:81
  99.6 279.3 %copy-start.12 = (bf16[2,16,16,128]{3,2,1,0:T(8,128)(2,1)S(1)}, bf16[2,16,16,128]{3,2,1,0:T(8,128)(2,1)}, u32[]{:S(2)}) copy-start(bf16[2,16,16,128]{3,2,1,0:T(8,128)(2,1)} %slice.1801) | copy-start | bytes 393220
  677.4 1.7 copy-start.7
  679.3 12.9 %copy-start.8 = (f32[432,432]{1,0:T(8,128)}, f32[432,432]{1,0:T(8,128)S(1)}, u32[]{:S(2)}) copy-start(f32[432,432]{1,0:T(8,128)S(1)} %fusion.25) | copy-start | bytes 2239492
  704.5 55.2 %copy-start.14 = (f32[3,128,128]{2,1,0:T(8,128)S(1)}, f32[3,128,128]{2,1,0:T(8,128)}, u32[]{:S(2)}) copy-start(f32[3,128,128]{2,1,0:T(8,128)} %custom-call.51) | copy-start | bytes 589828
  728.2 37.8 %copy-start.13 = (f32[128,80]{1,0:T(8,128)S(1)}, f32[128,80]{1,0:T(8,128)}, u32[]{:S(2)}) copy-start(f32[128,80]{1,0:T(8,128)} %pad_convert_fusion) | copy-start | bytes 122884
  805.7 4.1 copy-start.9
Sparse Core Ops, SparseCore 0:
  10.6 106.8 all-reduce.7
  122.1 87.7 reduce-scatter.4
  214.8 163.9 reduce-scatter.2
  381.5 270.1 all-reduce.9
